TPU v7x, 768 devices: a whole 4x8x12 slice. The times are simulated.
768 devices in a mesh: curve: 96 (over z, y), near: 8 (over x, core).
Axes of the slice: x: 4, y: 8, z: 12, core: 2. Of those that a mesh axis runs over, the one named last changes fastest.
Arguments:
- moments: float32 [84, 98304], P(None, ('curve', 'near')), may hold values from -6 to 6
- leaf_source: int32 [189, 98304], P(None, ('curve', 'near')), may hold values from 0 to 383, as said below
- leaf_mask: int32 [189, 98304], P(None, ('curve', 'near')), may hold values 0 or 1
- coarse_source: int32 [189, 1536], P(None, ('curve', 'near')), may hold values from 0 to 5, as said below
- up_shift: float32 [84, 84, 8], replicated, may hold values from -0.25 to 0.25
- down_shift: float32 [84, 84, 8], replicated, may hold values from -0.625 to 0.625
- far_shift: float32 [84, 84, 189], replicated, may hold values from -0.046875 to 0.046875
Outputs:
- field_local: float32 [84, 98304], P(None, ('curve', 'near'))
Inputs may be any that keep to these rules, and one draw needn't show every extreme that they name: `leaf_source`: every source is a leaf of the cell's own block of 128 leaves or of the block just before or after it along the curve, never outside the 98304 leaves: leaves of the first block use values of 128 or more, leaves of the last block values under 2 * 128. `coarse_source`: every source is a coarse cell of the cell's own block of 2 coarse cells or of the block just before or after it along the curve, never outside the 1536 cells: cells of the first block use values of 2 or more, cells of the last block values under 2 * 2.
All inputs are finite; a program needn't handle non-finite values. No bound on the sum of `leaf_mask` on one device may be relied on, other than what follows from the above.
Results may differ from a plain program's by a relative error of at most 0.000058.
Values sent between devices are 32-bit elements; how exact they have to be, the bound alone decides.
A program may use at most 64 MiB of HBM per device.

v0:
```python
import jax, jax.numpy as jnp
from jax import lax
from jax.experimental import pallas as pl
from jax.sharding import PartitionSpec
from jax.experimental.pallas import tpu as pltpu
BF, F32 = jnp.bfloat16, jnp.float32
HIGH = lax.Precision.HIGHEST
MESH = pl.DeviceIdType.MESH
P, K, C = 84, 189, 128
G = 7
NG = P // G

def split(v):
    hi = v.astype(BF)
    return hi, (v - hi.astype(F32)).astype(BF)

def tail(v):
    return jnp.concatenate([v, jnp.zeros((v.shape[0], 2 * 128 - K), v.dtype)], axis=1)

def kernel(m_hbm, src_hbm, msk_hbm, cs_hbm, up_hbm, dn_hbm, far_hbm, out_ref,
           win, cwin, src, msk, cs, up, dn, f32, fc, x0, x1, z, acc,
           sem, fsem, send, recv):
    nc, nn = lax.axis_size("curve"), lax.axis_size("near")
    n = nc * nn
    me = lax.axis_index("curve") * nn + lax.axis_index("near")
    def at(i):
        i = lax.rem(i + n, n)
        return (i // nn, lax.rem(i, nn))
    left, right = at(me - 1), at(me + 1)
    bar = pltpu.get_barrier_semaphore()
    for d in (left, right):
        pl.semaphore_signal(bar, inc=1, device_id=d, device_id_type=MESH)
    own = pltpu.make_async_copy(m_hbm, win.at[1], sem.at[0])
    own.start()
    upc = pltpu.make_async_copy(up_hbm, up, sem.at[1]); upc.start()
    src[184:192, :] = jnp.zeros((8, C), jnp.int32)
    msk[184:192, :] = jnp.zeros((8, C), jnp.int32)
    small = [pltpu.make_async_copy(src_hbm, src.at[0:K], sem.at[2]), pltpu.make_async_copy(msk_hbm, msk.at[0:K], sem.at[3]),
             pltpu.make_async_copy(cs_hbm, cs, sem.at[4]), pltpu.make_async_copy(dn_hbm, dn, sem.at[5])]
    def fcopy(q):
        return pltpu.make_async_copy(far_hbm.at[:, q, :], f32.at[q], fsem.at[q])
    def fstart(q, c):
        fcopy(q).start()
        return c
    lax.fori_loop(0, P, fstart, 0)
    for s in small: s.start()
    lane = lax.broadcasted_iota(jnp.int32, (P, C), 1)
    def pick(which):
        y = jnp.zeros((P, C), F32)
        for o in range(8):
            y = jnp.where(which == o, z[pl.ds(o, P, stride=8), :], y)
        return y
    def apply(op, x):
        z[...] = jnp.dot(op[...].reshape(8 * P, P), x, precision=HIGH, preferred_element_type=F32)
    own.wait(); upc.wait()
    apply(up, win[1])
    y = pick(lane % 8)
    for s in (1, 2, 4):
        y = y + pltpu.roll(y, C - s, 1)
    apply(up, y)
    y = pick(jnp.where(lane % 8 == 0, (lane // 8) % 8, -1))
    for s in (8, 16, 32):
        y = y + pltpu.roll(y, C - s, 1)
    cwin[1] = y
    pl.semaphore_wait(bar, 2)
    copies = []
    for j, buf in enumerate((win, cwin)):
        for i, (slot, d) in enumerate(((2, left), (0, right))):
            c = pltpu.make_async_remote_copy(src_ref=buf.at[1], dst_ref=buf.at[slot], send_sem=send.at[2*j+i], recv_sem=recv.at[2*j+i], device_id=d, device_id_type=MESH)
            c.start()
            copies.append(c)
    x1[...] = jnp.zeros_like(x1)
    x0[:, 192:256, :] = jnp.zeros((G, 64, 256), BF)
    lb = lax.broadcasted_iota(jnp.int32, (P, 128), 1) < K - 128
    def fsplit(q, c):
        fcopy(q).wait()
        a = f32[q, :, 0:128]
        b = tail(f32[q, :, 128:K])
        for t, v in enumerate((a, b)):
            hi, lo = split(v)
            l = pl.ds(pl.multiple_of(q * 256 + t * 128, 128), 128)
            fc[0, 0:P, l] = hi
            fc[1, 0:P, l] = lo
        return c
    lax.fori_loop(0, P, fsplit, 0, unroll=2)
    acc[...] = jnp.zeros_like(acc)
    for s in small: s.wait()
    for c in copies: c.wait()
    def gather(g, x):
        for t in range(12):
            r = slice(16 * t, 16 * t + 16)
            s, m = src[r, :], msk[r, :]
            idx = jnp.bitwise_and(s, 127)
            live = m > 0
            ms = ((s < 128) & live, (s >= 128) & (s < 256) & live, (s >= 256) & live)
            for j in range(G):
                v = jnp.zeros((16, C), F32)
                for b in range(3):
                    w = jnp.broadcast_to(win[b, pl.ds(g * G + j, 1), :], (16, C))
                    v = jnp.where(ms[b], jnp.take_along_axis(w, idx, axis=1, mode="promise_in_bounds"), v)
                x[j, r, 0:C], x[j, r, C:2*C] = split(v)
    def product(g, x):
        l = pl.ds(pl.multiple_of(g * (G * 256), 128), G * 256)
        acc[...] += jnp.dot(fc[:, :, l].reshape(192, G * 256), x[...].reshape(G * 256, 256), preferred_element_type=F32)
    def body(i, c):
        product(jnp.maximum(2 * i - 1, 0), x1)
        gather(2 * i, x0)
        product(2 * i, x0)
        gather(2 * i + 1, x1)
        return c
    lax.fori_loop(0, NG // 2, body, 0)
    product(NG - 1, x1)
    total = acc[0:P, 0:C] + (acc[0:P, C:2*C] + (acc[96:96+P, 0:C] + acc[96:96+P, C:2*C]))
    w = jnp.where(lane % 64 == 0, cwin[0], jnp.where(lane % 64 == 1, pltpu.roll(cwin[1], 1, 1), pltpu.roll(cwin[2], 2, 1)))
    for m in range(2):
        for t in range(2):
            s = tail(cs[m:m+1, 128:K]) if t else cs[m:m+1, 0:128]
            idx = jnp.bitwise_and((s & 1) * 64 + (s >> 1), 127)
            xc = jnp.take_along_axis(w, jnp.broadcast_to(idx, (P, C)), axis=1, mode="promise_in_bounds")
            if t:
                xc = jnp.where(lb, xc, 0.0)
            z[(2*m+t)*P:(2*m+t+1)*P, :] = xc
    def cstep(q, a):
        fa, fb = f32[q, :, 0:128], tail(f32[q, :, 128:K])
        return tuple(a[m] + fa * z[pl.ds(2*m*P + q, 1), :] + fb * z[pl.ds((2*m+1)*P + q, 1), :] for m in range(2))
    zero = jnp.zeros((P, C), F32)
    a = lax.fori_loop(0, P, cstep, (zero, zero), unroll=4)
    cl = jnp.where(lane < 64, jnp.sum(a[0], axis=1, keepdims=True), jnp.sum(a[1], axis=1, keepdims=True))
    apply(dn, cl)
    mid = pick((lane // 8) % 8)
    apply(dn, mid)
    total = total + pick(lane % 8)
    out_ref[...] = total

def run(moments, leaf_source, leaf_mask, coarse_source, up_shift, down_shift, far_shift):
    anyspec = pl.BlockSpec(memory_space=pl.ANY)
    V = pltpu.VMEM
    return pl.pallas_call(
        kernel,
        out_shape=jax.ShapeDtypeStruct((P, C), F32),
        in_specs=[anyspec] * 7,
        out_specs=pl.BlockSpec(memory_space=pltpu.VMEM),
        scratch_shapes=[
            V((3, P, C), F32), V((3, P, C), F32), V((192, C), jnp.int32), V((192, C), jnp.int32), V((2, K), jnp.int32),
            V((P, 8, P), F32), V((P, 8, P), F32), V((P, P, K), F32), V((2, 96, P * 256), BF), V((G, 256, 256), BF), V((G, 256, 256), BF),
            V((8 * P, C), F32), V((192, 256), F32),
            pltpu.SemaphoreType.DMA((6,)), pltpu.SemaphoreType.DMA((P,)), pltpu.SemaphoreType.DMA((4,)), pltpu.SemaphoreType.DMA((4,)),
        ],
        compiler_params=pltpu.CompilerParams(vmem_limit_bytes=56 << 20, collective_id=0, has_side_effects=True),
    )(moments, leaf_source, leaf_mask, coarse_source.T, jnp.transpose(up_shift, (0, 2, 1)), jnp.transpose(down_shift, (0, 2, 1)), far_shift)


def solution(mesh):
    cells = PartitionSpec(None, ("curve", "near"))
    copied = PartitionSpec()
    return jax.shard_map(run, mesh=mesh, in_specs=(cells,) * 4 + (copied,) * 3, out_specs=cells, check_vma=False)
```

profile of v0, /device:TPU:1, one launch (start us, length us, event | category | flops | bytes accessed | tf_op | source)
XLA Modules:
  0.0 39.3 jit_solution(11883961750513871618)
XLA Ops:
  0.0 37.9 %shard_map.73 = f32[84,128]{1,0:T(8,128)} custom-call(f32[84,128]{1,0:T(8,128)} %m_hbm.1, s32[189,128]{1,0:T(8,128)} %src_hbm.1, s32[189,128]{1,0:T(8,128)} %msk_hbm.1, s32[2,189]{1,0:T(2,128)} %bitcast.5, f32[84,8,84]{2,1,0:T(8,128)} %bitcast.3, f32[84,8,84]{2,1,0:T(8,128)} %bitcast.4, f32[84,84,189]{2,1,0:T(8,128)} %far_hbm.1), custom_call_target="tpu_custom_call" | custom-call | tf_op jit(solution)/shard_map/pallas_call | solution.py:138
  37.9 1.4 %copy.9 = f32[84,128]{1,0:T(8,128)} copy(f32[84,128]{1,0:T(8,128)} %shard_map.73) | data formatting | bytes 86016
where the time goes:
time: 39.5 us; the launch traced here: 39.3 us
  Pallas kernels  37.9 us (96%)
  local copies, waits for them, and re-layouts  1.41 us (4%)
    pallas_call x1, Pallas kernels, run(): pl.pallas_call(kernel, out_shape=jax.ShapeDtypeStruct((P, C), F32), in_sp...  37.9 us
    unnamed x1, local copies, waits for them, and re-layouts  1.41 us

commit v1 on v0

v1 whole, which is shorter than its diff:
```python
import jax, jax.numpy as jnp
from jax import lax
from jax.experimental import pallas as pl
from jax.experimental.pallas import tpu as pltpu
from jax.sharding import PartitionSpec
BF, F32, I32 = jnp.bfloat16, jnp.float32, jnp.int32
MESH = pl.DeviceIdType.MESH
P, K, C = 84, 189, 128
LO = 96
FC = 7
FW = 14


def rounded(v):
    return v.astype(BF).astype(F32)


def split(v):
    hi = v.astype(BF)
    return hi, (v - hi.astype(F32)).astype(BF)


def tail(v):
    return jnp.concatenate([v, jnp.zeros((v.shape[0], 2 * 128 - K), v.dtype)], axis=1)


def lanes(rows):
    return lax.broadcasted_iota(I32, (rows, C), 1)


def take(v, index):
    return jnp.take_along_axis(v, index, axis=1, mode="promise_in_bounds")


def kernel(m_hbm, src_hbm, msk_hbm, cs_hbm, up_hbm, dn_hbm, far_hbm, out_ref,
           win, cwin, src, msk, cs, up, dn, u3, d3, rr, z, f32, fw, fc, xp, xx, xc, ca, acc,
           sem, fsem, send, recv):
    nn = lax.axis_size("near")
    n = lax.axis_size("curve") * nn
    me = lax.axis_index("curve") * nn + lax.axis_index("near")
    early = lax.rem(me, 2) == 0
    has = (me > 0, me < n - 1)
    bar = pltpu.get_barrier_semaphore()

    def at(i):
        i = lax.rem(i + n, n)
        return (i // nn, lax.rem(i, nn))

    ends = (at(me - 1), at(me + 1))
    for side in range(2):
        @pl.when(has[side])
        def _():
            pl.semaphore_signal(bar, inc=1, device_id=ends[side], device_id_type=MESH)

    def remote(j, side):
        buf = (win, cwin)[j]
        return pltpu.make_async_remote_copy(
            src_ref=buf.at[1], dst_ref=buf.at[2 - 2 * side], send_sem=send.at[2 * j + side],
            recv_sem=recv.at[2 * j + 1 - side], device_id=ends[side], device_id_type=MESH)

    def each(cond, sides, act):
        for side in sides:
            @pl.when(jnp.logical_and(cond, has[side]))
            def _():
                act(side)

    def meet(cond):
        @pl.when(cond)
        def _():
            pl.semaphore_wait(bar, has[0].astype(I32) + has[1].astype(I32))

    own = pltpu.make_async_copy(m_hbm, win.at[1], sem.at[0])
    upc = pltpu.make_async_copy(up_hbm, up, sem.at[1])
    own.start()
    upc.start()
    src[184:192, :] = jnp.zeros((8, C), I32)
    msk[184:192, :] = jnp.zeros((8, C), I32)
    small = [pltpu.make_async_copy(a, b, sem.at[2 + i]) for i, (a, b) in enumerate(
        ((src_hbm, src.at[0:K]), (msk_hbm, msk.at[0:K]), (cs_hbm, cs), (dn_hbm, dn)))]

    def fcopy(q):
        return pltpu.make_async_copy(far_hbm.at[:, q, :], f32.at[q], fsem.at[lax.div(q, FW)])

    def fstart(q, c):
        fcopy(q).start()
        return c

    lax.fori_loop(0, P, fstart, 0)
    for s in small:
        s.start()
    lane = lanes(P)
    rr[248:256, :] = jnp.zeros((8, C), F32)

    def triple(dst, op):
        v = op[...].reshape(8 * P, P)
        hi = rounded(v)
        dst[...] = jnp.concatenate([hi, hi, v - hi, jnp.zeros((8 * P, 4), F32)], axis=1)

    def apply(op3, x):
        hi = rounded(x)
        rr[0:P, :] = hi
        rr[P:2 * P, :] = x - hi
        rr[2 * P:3 * P, :] = hi
        z[...] = jnp.dot(op3[...], rr[...], preferred_element_type=F32)

    def pick(which):
        y = jnp.zeros((P, C), F32)
        for o in range(8):
            y = jnp.where(which == o, z[pl.ds(o, P, stride=8), :], y)
        return y

    own.wait()
    meet(early)
    each(early, (0, 1), lambda side: remote(0, side).start())
    for side in range(2):
        @pl.when(jnp.logical_not(has[side]))
        def _():
            win[2 * side] = jnp.zeros((P, C), F32)
            cwin[2 * side] = jnp.zeros((P, C), F32)
    upc.wait()
    triple(u3, up)
    apply(u3, win[1])
    y = pick(lane % 8)
    for s in (1, 2, 4):
        y = y + pltpu.roll(y, C - s, 1)
    apply(u3, y)
    y = pick(jnp.where(lane % 8 == 0, (lane // 8) % 8, -1))
    for s in (8, 16, 32):
        y = y + pltpu.roll(y, C - s, 1)
    cwin[1] = y
    each(early, (0, 1), lambda side: remote(1, side).start())
    for s in small:
        s.wait()

    def gather(b, store, part, beside=None):
        def body(t, c):
            r = pl.ds(pl.multiple_of(t * 16, 16), 16)
            s, m = src[r, :], msk[r, :]
            index = jnp.bitwise_and(s, 127)
            hit = jnp.logical_and(lax.shift_right_logical(s, 7) == b, m > 0)
            if beside is not None:
                beside(t)
            for q in range(P):
                v = xp[q, r, :] if part else jnp.zeros((16, C), F32)
                w = jnp.broadcast_to(win[b, pl.ds(q, 1), :], (16, C))
                store(q, r, jnp.where(hit, take(w, index), v))
            return c
        lax.fori_loop(0, 12, body, 0)

    def whole(q, r, v):
        xp[q, r, :] = v

    def halves(q, r, v):
        xx[q, r, 0:C], xx[q, r, C:2 * C] = split(v)

    acc[...] = jnp.zeros_like(acc)
    xx[:, 192:256, :] = jnp.zeros((P, 64, 256), BF)
    triple(d3, dn)

    def fsplit(t):
        @pl.when(lax.rem(t, 2) == 0)
        def _():
            pltpu.make_async_copy(fw, fw, fsem.at[lax.div(t, 2)]).wait()

        for j in range(FC):
            q = t * FC + j
            for i, v in enumerate((f32[q, :, 0:128], tail(f32[q, :, 128:K]))):
                l = pl.ds(pl.multiple_of(q * 256 + i * 128, 128), 128)
                fc[0:P, l], fc[LO:LO + P, l] = split(v)

    gather(1, whole, False, fsplit)
    def coarse_sources():
        w = jnp.where(lane % 64 == 0, cwin[0], jnp.where(lane % 64 == 1, pltpu.roll(cwin[1], 1, 1), pltpu.roll(cwin[2], 2, 1)))
        for m in range(2):
            for t in range(2):
                s = tail(cs[m:m + 1, 128:K]) if t else cs[m:m + 1, 0:128]
                index = jnp.bitwise_and(jnp.bitwise_and(s, 1) * 64 + lax.shift_right_logical(s, 1), 127)
                x = take(w, jnp.broadcast_to(index, (P, C)))
                for q in range(P):
                    xc[2 * m + t, q] = jnp.broadcast_to(x[q:q + 1, :], (8, C))
        ca[...] = jnp.zeros_like(ca)

    def coarse(t):
        for i in range(11):
            r = slice(8 * i, min(8 * i + 8, P))
            n = r.stop - r.start
            sums = [ca[m, r, :] for m in range(2)]
            for j in range(FC):
                q = t * FC + j
                fa, fb = f32[q, r, 0:128], tail(f32[q, r, 128:K])
                for m in range(2):
                    sums[m] = sums[m] + fa * xc[2 * m, q, 0:n, :] + fb * xc[2 * m + 1, q, 0:n, :]
            for m in range(2):
                ca[m, r, :] = sums[m]

    late = jnp.logical_not(early)
    odd_one = me == 1
    send_both = lambda side: (remote(0, side).start(), remote(1, side).start())
    others = jnp.logical_and(late, jnp.logical_not(odd_one))
    meet(others)
    each(others, (0, 1), send_both)
    b1 = jnp.where(odd_one, 2, 0)
    each(odd_one, (1,), lambda side: remote(0, 1 - side).wait_recv())
    each(jnp.logical_not(odd_one), (0,), lambda side: remote(0, 1 - side).wait_recv())
    gather(b1, whole, True)
    meet(odd_one)
    each(odd_one, (0, 1), send_both)
    each(odd_one, (0,), lambda side: remote(0, 1 - side).wait_recv())
    each(jnp.logical_not(odd_one), (1,), lambda side: remote(0, 1 - side).wait_recv())
    each(True, (0, 1), lambda side: remote(1, 1 - side).wait_recv())
    coarse_sources()
    gather(2 - b1, halves, True, coarse)
    acc[...] = jnp.dot(fc[...], xx[...].reshape(P * 256, 256), preferred_element_type=F32)
    cl = jnp.where(lane < 64, *(jnp.sum(ca[m], axis=1, keepdims=True) for m in range(2)))
    apply(d3, cl)
    apply(d3, pick((lane // 8) % 8))
    far = acc[0:P, 0:C] + (acc[0:P, C:2 * C] + (acc[LO:LO + P, 0:C] + acc[LO:LO + P, C:2 * C]))
    out_ref[...] = far + pick(lane % 8)
    each(True, (0, 1), lambda side: (remote(0, side).wait_send(), remote(1, side).wait_send()))


def run(moments, leaf_source, leaf_mask, coarse_source, up_shift, down_shift, far_shift):
    V = pltpu.VMEM
    D = pltpu.SemaphoreType.DMA
    return pl.pallas_call(
        kernel,
        out_shape=jax.ShapeDtypeStruct((P, C), F32),
        in_specs=[pl.BlockSpec(memory_space=pl.ANY)] * 7,
        out_specs=pl.BlockSpec(memory_space=pltpu.VMEM),
        scratch_shapes=[
            V((3, P, C), F32), V((3, P, C), F32), V((192, C), I32), V((192, C), I32), V((2, K), I32),
            V((P, 8, P), F32), V((P, 8, P), F32), V((8 * P, 256), F32), V((8 * P, 256), F32), V((256, C), F32), V((8 * P, C), F32),
            V((P, P, K), F32), V((P * FW // 8, 8, K), F32), V((2 * LO, P * 256), BF), V((P, 192, C), F32), V((P, 256, 256), BF),
            V((4, P, 8, C), F32), V((2, P, C), F32), V((2 * LO, 256), F32),
            D((6,)), D((P // FW,)), D((4,)), D((4,)),
        ],
        compiler_params=pltpu.CompilerParams(vmem_limit_bytes=58 << 20, collective_id=0, has_side_effects=True),
    )(moments, leaf_source, leaf_mask, coarse_source.T, jnp.transpose(up_shift, (0, 2, 1)), jnp.transpose(down_shift, (0, 2, 1)), far_shift)


def solution(mesh):
    cells = PartitionSpec(None, ("curve", "near"))
    copied = PartitionSpec()
    return jax.shard_map(run, mesh=mesh, in_specs=(cells,) * 4 + (copied,) * 3, out_specs=cells, check_vma=False)
```

time: 39.5 us -> 30.5 us (0.77)
  the two profiles are of different devices: /device:TPU:1 before, /device:TPU:512 now
where the time goes in v1:
time: 30.5 us; the launch traced here: 30.3 us
  Pallas kernels  28.9 us (95%)
  local copies, waits for them, and re-layouts  1.41 us (5%)
    pallas_call x1, Pallas kernels, run(): pl.pallas_call(kernel, out_shape=jax.ShapeDtypeStruct((P, C), F32), in_sp...  28.9 us
    unnamed x1, local copies, waits for them, and re-layouts  1.41 us

profile of v1, /device:TPU:512, one launch (start us, length us, event | category | flops | bytes accessed | tf_op | source)
XLA Modules:
  0.0 30.3 jit_solution(10420007589982422706)
XLA Ops:
  0.0 28.9 %shard_map.73 = f32[84,128]{1,0:T(8,128)} custom-call(f32[84,128]{1,0:T(8,128)} %m_hbm.1, s32[189,128]{1,0:T(8,128)} %src_hbm.1, s32[189,128]{1,0:T(8,128)} %msk_hbm.1, s32[2,189]{1,0:T(2,128)} %bitcast.5, f32[84,8,84]{2,1,0:T(8,128)} %bitcast.3, f32[84,8,84]{2,1,0:T(8,128)} %bitcast.4, f32[84,84,189]{2,1,0:T(8,128)} %far_hbm.1), custom_call_target="tpu_custom_call" | custom-call | tf_op jit(solution)/shard_map/pallas_call | solution.py:225
  28.9 1.4 %copy.9 = f32[84,128]{1,0:T(8,128)} copy(f32[84,128]{1,0:T(8,128)} %shard_map.73) | data formatting | bytes 86016

commit v2 on v1

--- a/solution.py
+++ b/solution.py
@@ -33,12 +33,11 @@
 
 
 def kernel(m_hbm, src_hbm, msk_hbm, cs_hbm, up_hbm, dn_hbm, far_hbm, out_ref,
-           win, cwin, src, msk, cs, up, dn, u3, d3, rr, z, f32, fw, fc, xp, xx, xc, ca, acc,
+           win, cwin, src, msk, cs, up, dn, u3, d3, rr, z, f32, fw, fa, fb, xp, xa, xb, xc, ca, acc,
            sem, fsem, send, recv):
     nn = lax.axis_size("near")
     n = lax.axis_size("curve") * nn
     me = lax.axis_index("curve") * nn + lax.axis_index("near")
-    early = lax.rem(me, 2) == 0
     has = (me > 0, me < n - 1)
     bar = pltpu.get_barrier_semaphore()
 
@@ -53,9 +52,8 @@
             pl.semaphore_signal(bar, inc=1, device_id=ends[side], device_id_type=MESH)
 
     def remote(j, side):
-        buf = (win, cwin)[j]
         return pltpu.make_async_remote_copy(
-            src_ref=buf.at[1], dst_ref=buf.at[2 - 2 * side], send_sem=send.at[2 * j + side],
+            src_ref=cwin.at[1] if j else m_hbm, dst_ref=(win, cwin)[j].at[2 - 2 * side], send_sem=send.at[2 * j + side],
             recv_sem=recv.at[2 * j + 1 - side], device_id=ends[side], device_id_type=MESH)
 
     def each(cond, sides, act):
@@ -73,6 +71,8 @@
     upc = pltpu.make_async_copy(up_hbm, up, sem.at[1])
     own.start()
     upc.start()
+    meet(me == 0)
+    each(me == 0, (0, 1), lambda side: remote(0, side).start())
     src[184:192, :] = jnp.zeros((8, C), I32)
     msk[184:192, :] = jnp.zeros((8, C), I32)
     small = [pltpu.make_async_copy(a, b, sem.at[2 + i]) for i, (a, b) in enumerate(
@@ -110,8 +110,6 @@
         return y
 
     own.wait()
-    meet(early)
-    each(early, (0, 1), lambda side: remote(0, side).start())
     for side in range(2):
         @pl.when(jnp.logical_not(has[side]))
         def _():
@@ -128,11 +126,14 @@
     for s in (8, 16, 32):
         y = y + pltpu.roll(y, C - s, 1)
     cwin[1] = y
-    each(early, (0, 1), lambda side: remote(1, side).start())
+    mid = me > 1
+    meet(mid)
+    each(mid, (0, 1), lambda side: (remote(0, side).start(), remote(1, side).start()))
+    each(me == 0, (0, 1), lambda side: remote(1, side).start())
     for s in small:
         s.wait()
 
-    def gather(b, store, part, beside=None):
+    def gather(b, steps, store, part, beside=None):
         def body(t, c):
             r = pl.ds(pl.multiple_of(t * 16, 16), 16)
             s, m = src[r, :], msk[r, :]
@@ -143,18 +144,22 @@
             for q in range(P):
                 v = xp[q, r, :] if part else jnp.zeros((16, C), F32)
                 w = jnp.broadcast_to(win[b, pl.ds(q, 1), :], (16, C))
-                store(q, r, jnp.where(hit, take(w, index), v))
+                store(q, t, r, jnp.where(hit, take(w, index), v))
             return c
-        lax.fori_loop(0, 12, body, 0)
-
-    def whole(q, r, v):
+        lax.fori_loop(*steps, body, 0)
+
+    def whole(q, t, r, v):
         xp[q, r, :] = v
 
-    def halves(q, r, v):
-        xx[q, r, 0:C], xx[q, r, C:2 * C] = split(v)
+    def halves_a(q, t, r, v):
+        xa[q, r, 0:C], xa[q, r, C:2 * C] = split(v)
+
+    def halves_b(q, t, r, v):
+        r = pl.ds(pl.multiple_of((t - 8) * 16, 16), 16)
+        xb[q, r, 0:C], xb[q, r, C:2 * C] = split(v)
 
     acc[...] = jnp.zeros_like(acc)
-    xx[:, 192:256, :] = jnp.zeros((P, 64, 256), BF)
+    xb[:, 64:C, :] = jnp.zeros((P, C - 64, 256), BF)
     triple(d3, dn)
 
     def fsplit(t):
@@ -164,11 +169,11 @@
 
         for j in range(FC):
             q = t * FC + j
-            for i, v in enumerate((f32[q, :, 0:128], tail(f32[q, :, 128:K]))):
-                l = pl.ds(pl.multiple_of(q * 256 + i * 128, 128), 128)
-                fc[0:P, l], fc[LO:LO + P, l] = split(v)
-
-    gather(1, whole, False, fsplit)
+            l = pl.ds(pl.multiple_of(q * C, C), C)
+            for f, v in ((fa, f32[q, :, 0:C]), (fb, tail(f32[q, :, C:K]))):
+                f[0:P, l], f[LO:LO + P, l] = split(v)
+
+    gather(1, (0, 12), whole, False, fsplit)
     def coarse_sources():
         w = jnp.where(lane % 64 == 0, cwin[0], jnp.where(lane % 64 == 1, pltpu.roll(cwin[1], 1, 1), pltpu.roll(cwin[2], 2, 1)))
         for m in range(2):
@@ -180,37 +185,38 @@
                     xc[2 * m + t, q] = jnp.broadcast_to(x[q:q + 1, :], (8, C))
         ca[...] = jnp.zeros_like(ca)
 
-    def coarse(t):
+    def beside_b(t):
+        t = t - 8
+        step = P // 4
+        l = pl.ds(pl.multiple_of(t * (step * C), C), step * C)
+        acc[...] += jnp.dot(fa[:, l], xa[pl.ds(t * step, step)].reshape(step * C, 2 * C), preferred_element_type=F32)
         for i in range(11):
             r = slice(8 * i, min(8 * i + 8, P))
             n = r.stop - r.start
             sums = [ca[m, r, :] for m in range(2)]
-            for j in range(FC):
-                q = t * FC + j
-                fa, fb = f32[q, r, 0:128], tail(f32[q, r, 128:K])
+            for j in range(step):
+                q = t * step + j
+                u, v = f32[q, r, 0:C], tail(f32[q, r, C:K])
                 for m in range(2):
-                    sums[m] = sums[m] + fa * xc[2 * m, q, 0:n, :] + fb * xc[2 * m + 1, q, 0:n, :]
+                    sums[m] = sums[m] + u * xc[2 * m, q, 0:n, :] + v * xc[2 * m + 1, q, 0:n, :]
             for m in range(2):
                 ca[m, r, :] = sums[m]
 
-    late = jnp.logical_not(early)
-    odd_one = me == 1
-    send_both = lambda side: (remote(0, side).start(), remote(1, side).start())
-    others = jnp.logical_and(late, jnp.logical_not(odd_one))
-    meet(others)
-    each(others, (0, 1), send_both)
-    b1 = jnp.where(odd_one, 2, 0)
-    each(odd_one, (1,), lambda side: remote(0, 1 - side).wait_recv())
-    each(jnp.logical_not(odd_one), (0,), lambda side: remote(0, 1 - side).wait_recv())
-    gather(b1, whole, True)
-    meet(odd_one)
-    each(odd_one, (0, 1), send_both)
-    each(odd_one, (0,), lambda side: remote(0, 1 - side).wait_recv())
-    each(jnp.logical_not(odd_one), (1,), lambda side: remote(0, 1 - side).wait_recv())
+    one = me == 1
+    rest = jnp.logical_not(one)
+    b1 = jnp.where(one, 2, 0)
+    each(one, (1,), lambda side: remote(0, 1 - side).wait_recv())
+    each(rest, (0,), lambda side: remote(0, 1 - side).wait_recv())
+    gather(b1, (0, 12), whole, True)
+    meet(one)
+    each(one, (0, 1), lambda side: (remote(0, side).start(), remote(1, side).start()))
+    each(one, (0,), lambda side: remote(0, 1 - side).wait_recv())
+    each(rest, (1,), lambda side: remote(0, 1 - side).wait_recv())
+    gather(2 - b1, (0, 8), halves_a, True)
     each(True, (0, 1), lambda side: remote(1, 1 - side).wait_recv())
     coarse_sources()
-    gather(2 - b1, halves, True, coarse)
-    acc[...] = jnp.dot(fc[...], xx[...].reshape(P * 256, 256), preferred_element_type=F32)
+    gather(2 - b1, (8, 12), halves_b, True, beside_b)
+    acc[...] += jnp.dot(fb[...], xb[...].reshape(P * C, 2 * C), preferred_element_type=F32)
     cl = jnp.where(lane < 64, *(jnp.sum(ca[m], axis=1, keepdims=True) for m in range(2)))
     apply(d3, cl)
     apply(d3, pick((lane // 8) % 8))
@@ -230,7 +236,7 @@
         scratch_shapes=[
             V((3, P, C), F32), V((3, P, C), F32), V((192, C), I32), V((192, C), I32), V((2, K), I32),
             V((P, 8, P), F32), V((P, 8, P), F32), V((8 * P, 256), F32), V((8 * P, 256), F32), V((256, C), F32), V((8 * P, C), F32),
-            V((P, P, K), F32), V((P * FW // 8, 8, K), F32), V((2 * LO, P * 256), BF), V((P, 192, C), F32), V((P, 256, 256), BF),
+            V((P, P, K), F32), V((P * FW // 8, 8, K), F32), V((2 * LO, P * C), BF), V((2 * LO, P * C), BF), V((P, 192, C), F32), V((P, C, 256), BF), V((P, C, 256), BF),
             V((4, P, 8, C), F32), V((2, P, C), F32), V((2 * LO, 256), F32),
             D((6,)), D((P // FW,)), D((4,)), D((4,)),
         ],

time: 30.5 us -> 25.8 us (0.85)
  the two profiles are of different devices: /device:TPU:512 before, /device:TPU:2 now
where the time goes in v2:
time: 25.8 us; the launch traced here: 25.7 us
  Pallas kernels  24.2 us (94%)
  local copies, waits for them, and re-layouts  1.41 us (5%)
    pallas_call x1, Pallas kernels, run(): pl.pallas_call(kernel, out_shape=jax.ShapeDtypeStruct((P, C), F32), in_sp...  24.2 us
    unnamed x1, local copies, waits for them, and re-layouts  1.41 us

profile of v2, /device:TPU:2, one launch (start us, length us, event | category | flops | bytes accessed | tf_op | source)
XLA Modules:
  0.0 25.7 jit_solution(7712230737077344725)
XLA Ops:
  0.0 24.2 %shard_map.73 = f32[84,128]{1,0:T(8,128)} custom-call(f32[84,128]{1,0:T(8,128)} %m_hbm.1, s32[189,128]{1,0:T(8,128)} %src_hbm.1, s32[189,128]{1,0:T(8,128)} %msk_hbm.1, s32[2,189]{1,0:T(2,128)} %bitcast.5, f32[84,8,84]{2,1,0:T(8,128)} %bitcast.3, f32[84,8,84]{2,1,0:T(8,128)} %bitcast.4, f32[84,84,189]{2,1,0:T(8,128)} %far_hbm.1), custom_call_target="tpu_custom_call" | custom-call | tf_op jit(solution)/shard_map/pallas_call | solution.py:231
  24.2 1.4 %copy.9 = f32[84,128]{1,0:T(8,128)} copy(f32[84,128]{1,0:T(8,128)} %shard_map.73) | data formatting | bytes 86016

commit v3 on v2

--- a/solution.py
+++ b/solution.py
@@ -203,14 +203,15 @@
                 ca[m, r, :] = sums[m]
 
     one = me == 1
-    rest = jnp.logical_not(one)
-    b1 = jnp.where(one, 2, 0)
-    each(one, (1,), lambda side: remote(0, 1 - side).wait_recv())
+    near_one = jnp.logical_or(one, me == 2)
+    rest = jnp.logical_not(near_one)
+    b1 = jnp.where(near_one, 2, 0)
+    each(near_one, (1,), lambda side: remote(0, 1 - side).wait_recv())
     each(rest, (0,), lambda side: remote(0, 1 - side).wait_recv())
     gather(b1, (0, 12), whole, True)
     meet(one)
     each(one, (0, 1), lambda side: (remote(0, side).start(), remote(1, side).start()))
-    each(one, (0,), lambda side: remote(0, 1 - side).wait_recv())
+    each(near_one, (0,), lambda side: remote(0, 1 - side).wait_recv())
     each(rest, (1,), lambda side: remote(0, 1 - side).wait_recv())
     gather(2 - b1, (0, 8), halves_a, True)
     each(True, (0, 1), lambda side: remote(1, 1 - side).wait_recv())
@@ -230,7 +231,7 @@
     D = pltpu.SemaphoreType.DMA
     return pl.pallas_call(
         kernel,
-        out_shape=jax.ShapeDtypeStruct((P, C), F32),
+        out_shape=V((P, C), F32),
         in_specs=[pl.BlockSpec(memory_space=pl.ANY)] * 7,
         out_specs=pl.BlockSpec(memory_space=pltpu.VMEM),
         scratch_shapes=[

time: 25.8 us -> 22.9 us (0.89)
  the two profiles are of different devices: /device:TPU:2 before, /device:TPU:512 now
where the time goes in v3:
time: 22.9 us; the launch traced here: 22.8 us
  Pallas kernels  22.2 us (97%)
  local copies, waits for them, and re-layouts  0.62 us (3%)
    pallas_call x1, Pallas kernels, run(): pl.pallas_call(kernel, out_shape=V((P, C), F32), in_specs=[pl.BlockSpec(m...  22.2 us
    unnamed x1, local copies, waits for them, and re-layouts  0.62 us

profile of v3, /device:TPU:512, one launch (start us, length us, event | category | flops | bytes accessed | tf_op | source)
XLA Modules:
  0.0 22.8 jit_solution(2590739115557067850)
XLA Ops:
  0.0 22.2 %shard_map.73 = f32[84,128]{1,0:T(8,128)S(1)} custom-call(f32[84,128]{1,0:T(8,128)} %m_hbm.1, s32[189,128]{1,0:T(8,128)} %src_hbm.1, s32[189,128]{1,0:T(8,128)} %msk_hbm.1, s32[2,189]{1,0:T(2,128)} %bitcast.5, f32[84,8,84]{2,1,0:T(8,128)} %bitcast.3, f32[84,8,84]{2,1,0:T(8,128)} %bitcast.4, f32[84,84,189]{2,1,0:T(8,128)} %far_hbm.1), custom_call_target="tpu_custom_call" | custom-call | tf_op jit(solution)/shard_map/pallas_call | solution.py:232
  22.2 0.6 %copy.9 = f32[84,128]{1,0:T(8,128)} copy(f32[84,128]{1,0:T(8,128)S(1)} %shard_map.73) | data formatting | bytes 86016

commit v4 on v3

--- a/solution.py
+++ b/solution.py
@@ -203,15 +203,15 @@
                 ca[m, r, :] = sums[m]
 
     one = me == 1
-    near_one = jnp.logical_or(one, me == 2)
-    rest = jnp.logical_not(near_one)
-    b1 = jnp.where(near_one, 2, 0)
-    each(near_one, (1,), lambda side: remote(0, 1 - side).wait_recv())
+    right_first = jnp.logical_or(one, lax.rem(me, 2) == 0)
+    rest = jnp.logical_not(right_first)
+    b1 = jnp.where(right_first, 2, 0)
+    each(right_first, (1,), lambda side: remote(0, 1 - side).wait_recv())
     each(rest, (0,), lambda side: remote(0, 1 - side).wait_recv())
     gather(b1, (0, 12), whole, True)
     meet(one)
     each(one, (0, 1), lambda side: (remote(0, side).start(), remote(1, side).start()))
-    each(near_one, (0,), lambda side: remote(0, 1 - side).wait_recv())
+    each(right_first, (0,), lambda side: remote(0, 1 - side).wait_recv())
     each(rest, (1,), lambda side: remote(0, 1 - side).wait_recv())
     gather(2 - b1, (0, 8), halves_a, True)
     each(True, (0, 1), lambda side: remote(1, 1 - side).wait_recv())

time: 22.9 us -> 22 us (0.961)
  Pallas kernels: 22.2 us -> 21.3 us
    pallas_call x1, Pallas kernels: 22.2 us -> 21.3 us  [run(): pl.pallas_call(kernel, out_shape=V((P, C), F32), in_specs=[pl.BlockSpec(m...]
where the time goes in v4:
time: 22 us; the launch traced here: 21.9 us
  Pallas kernels  21.3 us (97%)
  local copies, waits for them, and re-layouts  0.62 us (3%)
    pallas_call x1, Pallas kernels, run(): pl.pallas_call(kernel, out_shape=V((P, C), F32), in_specs=[pl.BlockSpec(m...  21.3 us
    unnamed x1, local copies, waits for them, and re-layouts  0.62 us

profile of v4, /device:TPU:512, one launch (start us, length us, event | category | flops | bytes accessed | tf_op | source)
XLA Modules:
  0.0 21.9 jit_solution(6845014713429449857)
XLA Ops:
  0.0 21.3 %shard_map.73 = f32[84,128]{1,0:T(8,128)S(1)} custom-call(f32[84,128]{1,0:T(8,128)} %m_hbm.1, s32[189,128]{1,0:T(8,128)} %src_hbm.1, s32[189,128]{1,0:T(8,128)} %msk_hbm.1, s32[2,189]{1,0:T(2,128)} %bitcast.5, f32[84,8,84]{2,1,0:T(8,128)} %bitcast.3, f32[84,8,84]{2,1,0:T(8,128)} %bitcast.4, f32[84,84,189]{2,1,0:T(8,128)} %far_hbm.1), custom_call_target="tpu_custom_call" | custom-call | tf_op jit(solution)/shard_map/pallas_call | solution.py:232
  21.3 0.6 %copy.9 = f32[84,128]{1,0:T(8,128)} copy(f32[84,128]{1,0:T(8,128)S(1)} %shard_map.73) | data formatting | bytes 86016
